TPU v7x, 128 devices: a whole 4x4x4 slice. The times are simulated.
128 devices in a mesh: dom: 32 (over x, z, core), grp: 4 (over y).
Axes of the slice: x: 4, y: 4, z: 4, core: 2. Of those that a mesh axis runs over, the one named last changes fastest.
Arguments:
- x_current: bfloat16 [524288, 128], P(('dom', 'grp')), may hold values from -6 to 6
- x_cached: bfloat16 [524288, 128], P(('dom', 'grp')), may hold values from -6 to 6
- w_self: bfloat16 [128, 512], replicated, may hold values from -0.5 to 0.5
- w_neigh: bfloat16 [128, 512], replicated, may hold values from -1 to 1
- bias: float32 [512], replicated, may hold values from -3 to 3
- tile_columns: int32 [4096, 40], P(('dom', 'grp')), may hold values from 0 to 255
- tile_count: int32 [4096], P(('dom', 'grp')), may hold values from 1 to 40, as said below
- adjacency: int32 [4096, 40, 2048], P(('dom', 'grp')), may hold values from 0 to 255, as said below
- degree: int32 [524288], P(('dom', 'grp')), may hold values from 1 to 5128, as said below
- boundary_blocks: int32 [128, 1], P(('dom', 'grp')), may hold values from 0 to 31
Outputs:
- hidden: bfloat16 [524288, 512], P(('dom', 'grp'))
Inputs may be any that keep to these rules, and one draw needn't show every extreme that they name: `tile_count`: every device has a row block with all 40 slots live. `adjacency`: 8 entries of a tile row packed into each word, bit b for column 8 c + b. `degree`: at least the number of ones in the row of the live tiles of the node's row block.
All inputs are finite; a program needn't handle non-finite values.
Results may differ from a plain program's by a relative error of at most 0.0025.
Values may be sent and summed in bfloat16 or wider, within the bound.
A program may use at most 192 MiB of HBM per device.

v0:
```python
import math
import jax
import jax.numpy as jnp
from jax import lax
from jax.sharding import PartitionSpec as P


def on_device(
    x_current,
    x_cached,
    w_self,
    w_neigh,
    bias,
    tile_columns,
    tile_count,
    adjacency,
    degree,
    boundary_blocks,
):
    node_rows, width = x_current.shape
    row_blocks, per_tile = tile_columns.shape
    tile_rows = node_rows // row_blocks
    chosen = x_cached.reshape(row_blocks, tile_rows, width)[boundary_blocks[0]]
    received = lax.all_gather(x_current, "grp", axis=0, tiled=True)
    part_blocks = received.reshape(-1, tile_rows, width)
    partial_value = lax.all_gather(chosen[None, None], "grp", axis=1, tiled=True)
    halo_blocks = lax.all_gather(partial_value, "dom", axis=0, tiled=True)
    block_table = jnp.concatenate([part_blocks, halo_blocks.reshape(-1, tile_rows, width)], axis=0)
    group_size = math.gcd(4, row_blocks)
    turns = row_blocks // group_size
    shifts = jnp.arange(8, dtype=jnp.int32)

    def one_group(pieces):
        columns, counts, packed = pieces
        bit_values = (
            packed.reshape(group_size, per_tile, tile_rows, tile_rows // 8, 1) >> shifts & 1
        )
        live_mask = (jnp.arange(per_tile, dtype=jnp.int32)[None, :] < counts[:, None]).astype(
            jnp.int32
        )
        adjacent = (
            bit_values.reshape(group_size, per_tile, tile_rows, tile_rows)
            * live_mask[:, :, None, None]
        ).astype(jnp.bfloat16)
        gathered = block_table[columns]
        return jnp.einsum("stij,stjf->sif", adjacent, gathered, preferred_element_type=jnp.float32)

    totals = lax.map(
        one_group,
        (
            tile_columns.reshape(turns, group_size, per_tile),
            tile_count.reshape(turns, group_size),
            adjacency.reshape(turns, group_size, per_tile, -1),
        ),
    )
    totals = totals.reshape(node_rows, width)
    average = (totals / degree.astype(jnp.float32)[:, None]).astype(jnp.bfloat16)
    summed = (
        jnp.dot(x_current, w_self, preferred_element_type=jnp.float32)
        + jnp.dot(average, w_neigh, preferred_element_type=jnp.float32)
        + bias
    )
    return jnp.maximum(summed, 0.0).astype(jnp.bfloat16)


def solution(mesh):
    in_specs = (
        P(("dom", "grp"), None),
        P(("dom", "grp"), None),
        P(),
        P(),
        P(),
        P(("dom", "grp"), None),
        P(("dom", "grp")),
        P(("dom", "grp"), None, None),
        P(("dom", "grp")),
        P(("dom", "grp"), None),
    )
    out_specs = P(("dom", "grp"), None)
    return jax.shard_map(
        on_device, mesh=mesh, in_specs=in_specs, out_specs=out_specs, check_vma=False
    )
```

profile of v0, /device:TPU:1, one launch (start us, length us, event | category | flops | bytes accessed | tf_op | source)
XLA Modules:
  0.0 343.1 jit_solution(17156375614477139263)
XLA Ops:
  8.0 11.2 %all-gather = bf16[4,128,128]{2,1,0:T(8,128)(2,1)} all-gather(bf16[1,128,128]{2,1,0:T(8,128)(2,1)S(1)} %constant_dynamic-slice_fusion.2), channel_id=2, replica_groups=mesh['dom'=32,'grp'=4] {'grp'}, dimensions={0}, use_global_device_ids=true | all-gather | bytes 163840 | tf_op jit(solution)/shard_map/all_gather | solution.py:26
  19.3 20.7 %copy.16 = s32[32,40,2048]{1,2,0:T(8,128)} copy(s32[32,40,2048]{2,1,0:T(8,128)} %param.19) | data formatting | bytes 20971520 | tf_op args[7]
  44.5 16.1 %all-gather.5.cloned.1.call-done = bf16[16384,128]{1,0:T(8,128)(2,1)} async-done(((bf16[4096,128]{1,0:T(8,128)(2,1)}), bf16[16384,128]{1,0:T(8,128)(2,1)}) %all-gather.5.cloned.1.call-update) | async-done | bytes 4194320 | tf_op jit(solution)/shard_map/all_gather | solution.py:24
  60.6 49.4 %all-gather.7.cloned.1.call-done = bf16[128,128,128]{2,1,0:T(8,128)(2,1)} async-done(((bf16[4,128,128]{2,1,0:T(8,128)(2,1)}), bf16[128,128,128]{2,1,0:T(8,128)(2,1)}) %all-gather.7.cloned.1.call-update) | async-done | bytes 4194320 | tf_op jit(solution)/shard_map/all_gather | solution.py:27
  110.0 7.4 %pad_maximum_fusion = bf16[256,128,128]{2,1,0:T(8,128)(2,1)} fusion(bf16[128,128,128]{2,1,0:T(8,128)(2,1)} %all-gather.7.cloned.1.call-done, bf16[128,128,128]{2,1,0:T(8,128)(2,1)} %bitcast.63), kind=kLoop, calls=%fused_computation.21 | loop fusion | flops 4194304 | bytes 16777216 | tf_op jit(solution)/shard_map/concatenate | solution.py:28
  117.4 210.2 %while.12 = (s32[]{:T(128)}, f32[8,4,128,128]{3,2,1,0:T(8,128)}, s32[8,4,40,2048]{2,3,1,0:T(8,128)}, s32[8,4]{1,0:T(8,128)S(1)}, s32[8,4,40]{2,1,0:T(4,128)}, /*index=5*/bf16[256,128,128]{2,1,0:T(8,128)(2,1)}, s32[]{:T(128)}) while((s32[]{:T(128)}, f32[8,4,128,128]{3,2,1,0:T(8,128)}, s32[8,4,40,2048]{2,3,1,0:T(8,128)}, ...), condition=%wide.region_1.2_spmd.clone, body=%wide.region_0.1_spmd.clone.sunk | while | flops 681576256 | bytes 22556296 | solution.py:48
  118.2 11.2 %gather_fusion = bf16[160,128,128]{2,1,0:T(8,128)(2,1)} fusion(bf16[256,128,128]{2,1,0:T(8,128)(2,1)} %get-tuple-element.136, s32[1024]{0:T(1024)S(1)} %pad_clamp_fusion.2), kind=kCustom, calls=%fused_computation.clone.clone.1 | custom fusion | bytes 10486400 | tf_op jit(solution)/shard_map/while/body/eval_jaxpr/gather | solution.py:45
  129.3 4.5 %constant_dynamic-slice_fusion.4 = s32[1,4,40,2048]{2,3,1,0:T(8,128)} fusion(s32[8,4,40,2048]{2,3,1,0:T(8,128)} %get-tuple-element.133, s32[]{:T(128)} %get-tuple-element.124), kind=kLoop, calls=%fused_computation.18.clone.1 | loop fusion | bytes 2621444 | tf_op jit(solution)/shard_map/while/body/jit(dynamic_index_in_dim)/dynamic_slice | solution.py:48
  137.4 6.3 %fusion.36 = f32[8,4,128,128]{3,2,1,0:T(8,128)} fusion(f32[8,4,128,128]{3,2,1,0:T(8,128)} %get-tuple-element.125, s32[]{:T(128)} %get-tuple-element.124, bf16[4,40,128,128]{3,2,1,0:T(8,128)(2,1)} %bitcast.61, s32[4,40]{1,0:T(4,128)S(1)} %fusion.35, s32[128]{0:T(128)S(1)} %shift_right_arithmetic.64, s32[4,40,128,16]{2,3,1,0:T(8,128)S(1)} %copy.20), kind=kOutput, calls=%fused_computation.12.clone.1 | convolution fusion | flops 681574400 | bytes 6817408 | tf_op jit(solution)/shard_map/while/body/eval_jaxpr/stij,stjf->sif/dot_general | solution.py:46
  144.4 11.2 %gather_fusion = bf16[160,128,128]{2,1,0:T(8,128)(2,1)} fusion(bf16[256,128,128]{2,1,0:T(8,128)(2,1)} %get-tuple-element.136, s32[1024]{0:T(1024)S(1)} %pad_clamp_fusion.2), kind=kCustom, calls=%fused_computation.clone.clone.1 | custom fusion | bytes 10486400 | tf_op jit(solution)/shard_map/while/body/eval_jaxpr/gather | solution.py:45
  163.7 6.3 %fusion.36 = f32[8,4,128,128]{3,2,1,0:T(8,128)} fusion(f32[8,4,128,128]{3,2,1,0:T(8,128)} %get-tuple-element.125, s32[]{:T(128)} %get-tuple-element.124, bf16[4,40,128,128]{3,2,1,0:T(8,128)(2,1)} %bitcast.61, s32[4,40]{1,0:T(4,128)S(1)} %fusion.35, s32[128]{0:T(128)S(1)} %shift_right_arithmetic.64, s32[4,40,128,16]{2,3,1,0:T(8,128)S(1)} %copy.20), kind=kOutput, calls=%fused_computation.12.clone.1 | convolution fusion | flops 681574400 | bytes 6817408 | tf_op jit(solution)/shard_map/while/body/eval_jaxpr/stij,stjf->sif/dot_general | solution.py:46
  170.7 11.2 %gather_fusion = bf16[160,128,128]{2,1,0:T(8,128)(2,1)} fusion(bf16[256,128,128]{2,1,0:T(8,128)(2,1)} %get-tuple-element.136, s32[1024]{0:T(1024)S(1)} %pad_clamp_fusion.2), kind=kCustom, calls=%fused_computation.clone.clone.1 | custom fusion | bytes 10486400 | tf_op jit(solution)/shard_map/while/body/eval_jaxpr/gather | solution.py:45
  189.9 6.3 %fusion.36 = f32[8,4,128,128]{3,2,1,0:T(8,128)} fusion(f32[8,4,128,128]{3,2,1,0:T(8,128)} %get-tuple-element.125, s32[]{:T(128)} %get-tuple-element.124, bf16[4,40,128,128]{3,2,1,0:T(8,128)(2,1)} %bitcast.61, s32[4,40]{1,0:T(4,128)S(1)} %fusion.35, s32[128]{0:T(128)S(1)} %shift_right_arithmetic.64, s32[4,40,128,16]{2,3,1,0:T(8,128)S(1)} %copy.20), kind=kOutput, calls=%fused_computation.12.clone.1 | convolution fusion | flops 681574400 | bytes 6817408 | tf_op jit(solution)/shard_map/while/body/eval_jaxpr/stij,stjf->sif/dot_general | solution.py:46
  197.0 11.2 %gather_fusion = bf16[160,128,128]{2,1,0:T(8,128)(2,1)} fusion(bf16[256,128,128]{2,1,0:T(8,128)(2,1)} %get-tuple-element.136, s32[1024]{0:T(1024)S(1)} %pad_clamp_fusion.2), kind=kCustom, calls=%fused_computation.clone.clone.1 | custom fusion | bytes 10486400 | tf_op jit(solution)/shard_map/while/body/eval_jaxpr/gather | solution.py:45
  216.2 6.3 %fusion.36 = f32[8,4,128,128]{3,2,1,0:T(8,128)} fusion(f32[8,4,128,128]{3,2,1,0:T(8,128)} %get-tuple-element.125, s32[]{:T(128)} %get-tuple-element.124, bf16[4,40,128,128]{3,2,1,0:T(8,128)(2,1)} %bitcast.61, s32[4,40]{1,0:T(4,128)S(1)} %fusion.35, s32[128]{0:T(128)S(1)} %shift_right_arithmetic.64, s32[4,40,128,16]{2,3,1,0:T(8,128)S(1)} %copy.20), kind=kOutput, calls=%fused_computation.12.clone.1 | convolution fusion | flops 681574400 | bytes 6817408 | tf_op jit(solution)/shard_map/while/body/eval_jaxpr/stij,stjf->sif/dot_general | solution.py:46
  223.2 11.2 %gather_fusion = bf16[160,128,128]{2,1,0:T(8,128)(2,1)} fusion(bf16[256,128,128]{2,1,0:T(8,128)(2,1)} %get-tuple-element.136, s32[1024]{0:T(1024)S(1)} %pad_clamp_fusion.2), kind=kCustom, calls=%fused_computation.clone.clone.1 | custom fusion | bytes 10486400 | tf_op jit(solution)/shard_map/while/body/eval_jaxpr/gather | solution.py:45
  242.4 6.3 %fusion.36 = f32[8,4,128,128]{3,2,1,0:T(8,128)} fusion(f32[8,4,128,128]{3,2,1,0:T(8,128)} %get-tuple-element.125, s32[]{:T(128)} %get-tuple-element.124, bf16[4,40,128,128]{3,2,1,0:T(8,128)(2,1)} %bitcast.61, s32[4,40]{1,0:T(4,128)S(1)} %fusion.35, s32[128]{0:T(128)S(1)} %shift_right_arithmetic.64, s32[4,40,128,16]{2,3,1,0:T(8,128)S(1)} %copy.20), kind=kOutput, calls=%fused_computation.12.clone.1 | convolution fusion | flops 681574400 | bytes 6817408 | tf_op jit(solution)/shard_map/while/body/eval_jaxpr/stij,stjf->sif/dot_general | solution.py:46
  249.5 11.2 %gather_fusion = bf16[160,128,128]{2,1,0:T(8,128)(2,1)} fusion(bf16[256,128,128]{2,1,0:T(8,128)(2,1)} %get-tuple-element.136, s32[1024]{0:T(1024)S(1)} %pad_clamp_fusion.2), kind=kCustom, calls=%fused_computation.clone.clone.1 | custom fusion | bytes 10486400 | tf_op jit(solution)/shard_map/while/body/eval_jaxpr/gather | solution.py:45
  268.7 6.3 %fusion.36 = f32[8,4,128,128]{3,2,1,0:T(8,128)} fusion(f32[8,4,128,128]{3,2,1,0:T(8,128)} %get-tuple-element.125, s32[]{:T(128)} %get-tuple-element.124, bf16[4,40,128,128]{3,2,1,0:T(8,128)(2,1)} %bitcast.61, s32[4,40]{1,0:T(4,128)S(1)} %fusion.35, s32[128]{0:T(128)S(1)} %shift_right_arithmetic.64, s32[4,40,128,16]{2,3,1,0:T(8,128)S(1)} %copy.20), kind=kOutput, calls=%fused_computation.12.clone.1 | convolution fusion | flops 681574400 | bytes 6817408 | tf_op jit(solution)/shard_map/while/body/eval_jaxpr/stij,stjf->sif/dot_general | solution.py:46
  275.8 11.2 %gather_fusion = bf16[160,128,128]{2,1,0:T(8,128)(2,1)} fusion(bf16[256,128,128]{2,1,0:T(8,128)(2,1)} %get-tuple-element.136, s32[1024]{0:T(1024)S(1)} %pad_clamp_fusion.2), kind=kCustom, calls=%fused_computation.clone.clone.1 | custom fusion | bytes 10486400 | tf_op jit(solution)/shard_map/while/body/eval_jaxpr/gather | solution.py:45
  295.0 6.3 %fusion.36 = f32[8,4,128,128]{3,2,1,0:T(8,128)} fusion(f32[8,4,128,128]{3,2,1,0:T(8,128)} %get-tuple-element.125, s32[]{:T(128)} %get-tuple-element.124, bf16[4,40,128,128]{3,2,1,0:T(8,128)(2,1)} %bitcast.61, s32[4,40]{1,0:T(4,128)S(1)} %fusion.35, s32[128]{0:T(128)S(1)} %shift_right_arithmetic.64, s32[4,40,128,16]{2,3,1,0:T(8,128)S(1)} %copy.20), kind=kOutput, calls=%fused_computation.12.clone.1 | convolution fusion | flops 681574400 | bytes 6817408 | tf_op jit(solution)/shard_map/while/body/eval_jaxpr/stij,stjf->sif/dot_general | solution.py:46
  302.1 11.2 %gather_fusion = bf16[160,128,128]{2,1,0:T(8,128)(2,1)} fusion(bf16[256,128,128]{2,1,0:T(8,128)(2,1)} %get-tuple-element.136, s32[1024]{0:T(1024)S(1)} %pad_clamp_fusion.2), kind=kCustom, calls=%fused_computation.clone.clone.1 | custom fusion | bytes 10486400 | tf_op jit(solution)/shard_map/while/body/eval_jaxpr/gather | solution.py:45
  321.3 6.3 %fusion.36 = f32[8,4,128,128]{3,2,1,0:T(8,128)} fusion(f32[8,4,128,128]{3,2,1,0:T(8,128)} %get-tuple-element.125, s32[]{:T(128)} %get-tuple-element.124, bf16[4,40,128,128]{3,2,1,0:T(8,128)(2,1)} %bitcast.61, s32[4,40]{1,0:T(4,128)S(1)} %fusion.35, s32[128]{0:T(128)S(1)} %shift_right_arithmetic.64, s32[4,40,128,16]{2,3,1,0:T(8,128)S(1)} %copy.20), kind=kOutput, calls=%fused_computation.12.clone.1 | convolution fusion | flops 681574400 | bytes 6817408 | tf_op jit(solution)/shard_map/while/body/eval_jaxpr/stij,stjf->sif/dot_general | solution.py:46
  329.6 6.6 %maximum_convert_fusion = bf16[4096,512]{1,0:T(8,128)(2,1)} fusion(f32[4096,512]{1,0:T(8,128)} %fusion.21, bf16[4096,128]{1,0:T(8,128)(2,1)S(1)} %fusion.20, bf16[128,512]{1,0:T(8,128)(2,1)S(1)} %copy-done.4, f32[512]{0:T(512)S(1)} %copy-done.6), kind=kOutput, calls=%fused_computation.22 | convolution fusion | flops 545259520 | bytes 13764608 | tf_op jit(solution)/shard_map/dot_general | solution.py:60
  (97 shorter events, 73.5 us)
Async XLA Ops:
  6.5 1.4 copy-start
  6.5 54.0 %all-gather.5.cloned.1.call-start = ((), (), s32[]{:S(2)}) async-start(), calls=%async_computation | async-start | bytes 5242880 | tf_op jit(solution)/shard_map/all_gather | solution.py:24
  7.3 102.7 %all-gather.7.cloned.1.call-start = ((), (), s32[]{:S(2)}) async-start(), calls=%async_computation.1 | async-start | bytes 4325376 | tf_op jit(solution)/shard_map/all_gather | solution.py:27
  19.2 20.7 %copy-start.7 = (s32[32]{0:T(128)S(1)}, s32[32]{0:T(128)}, u32[]{:S(2)}) copy-start(s32[32]{0:T(128)} %param.18) | copy-start | bytes 388
  19.2 20.8 %copy-start.5 = (s32[4096]{0:T(1024)S(1)}, s32[4096]{0:T(1024)}, u32[]{:S(2)}) copy-start(s32[4096]{0:T(1024)} %param.20) | copy-start | bytes 49156
  19.2 20.8 %copy-start.2 = (bf16[4096,128]{1,0:T(8,128)(2,1)S(1)}, bf16[4096,128]{1,0:T(8,128)(2,1)}, u32[]{:S(2)}) copy-start(bf16[4096,128]{1,0:T(8,128)(2,1)} %param.12) | copy-start | bytes 3145732
  19.2 20.8 %copy-start.3 = (bf16[128,512]{1,0:T(8,128)(2,1)S(1)}, bf16[128,512]{1,0:T(8,128)(2,1)}, u32[]{:S(2)}) copy-start(bf16[128,512]{1,0:T(8,128)(2,1)} %param.14) | copy-start | bytes 393220
  117.4 212.2 %copy-start.4 = (bf16[128,512]{1,0:T(8,128)(2,1)S(1)}, bf16[128,512]{1,0:T(8,128)(2,1)}, u32[]{:S(2)}) copy-start(bf16[128,512]{1,0:T(8,128)(2,1)} %param.15) | copy-start | bytes 393220
  117.4 212.2 %copy-start.6 = (f32[512]{0:T(512)S(1)}, f32[512]{0:T(512)}, u32[]{:S(2)}) copy-start(f32[512]{0:T(512)} %param.16) | copy-start | bytes 6148
  327.5 8.7 %copy-start.1 = (bf16[4096,128]{1,0:T(8,128)(2,1)S(1)}, bf16[4096,128]{1,0:T(8,128)(2,1)}, u32[]{:S(2)}) copy-start(bf16[4096,128]{1,0:T(8,128)(2,1)} %param.13) | copy-start | bytes 3145732
Sparse Core Ops, SparseCore 0:
  9.0 51.4 all-gather.4
  62.8 47.1 all-gather.6
where the time goes:
time: 345 us; the launch traced here: 343 us
  local copies, waits for them, and re-layouts  174 us (50%)
  waiting for transfers between devices  66.2 us (19%)
  matrix products  61.2 us (18%)
  other arithmetic  15.6 us (5%)
  between operations  14.2 us (4%)
  blocking collectives  11.2 us (3%)
    gather x8, local copies, waits for them, and re-layouts, one_group(): gathered = block_table[columns]  89.3 us
    dot_general x8, matrix products, one_group(): jnp.einsum('stij,stjf->sif', adjacent, gathered, preferred_element_type=j...  50.2 us
    all_gather x1, waiting for transfers between devices, on_device(): halo_blocks = lax.all_gather(partial_value, 'dom', axis=0, tiled=True)  49.4 us
    dynamic_slice x8, local copies, waits for them, and re-layouts, on_device(): lax.map(one_group, (tile_columns.reshape(turns, group_size, per_tile), ti...  35.8 us
    shift_right_arithmetic x24, local copies, waits for them, and re-layouts, one_group(): packed.reshape(group_size, per_tile, tile_rows, tile_rows // 8, 1) >> shifts  27.9 us
    unnamed x17, local copies, waits for them, and re-layouts  20.7 us
    all_gather x1, waiting for transfers between devices, on_device(): received = lax.all_gather(x_current, 'grp', axis=0, tiled=True)  16.1 us
    all_gather x1, blocking collectives, on_device(): lax.all_gather(chosen[None, None], 'grp', axis=1, tiled=True)  11.2 us
  transfers between devices with their start and end apart: 2, of which 2 were waited for; matrix products, arithmetic and copies ran while one was open for 7% of the time, Pallas kernels for 0%

commit v1 on v0

--- a/solution.py
+++ b/solution.py
@@ -3,6 +3,19 @@
 import jax.numpy as jnp
 from jax import lax
 from jax.sharding import PartitionSpec as P
+
+
+def collect(value, axis, dim):
+    ways = lax.axis_size(axis)
+    up = [(d, (d + 1) % ways) for d in range(ways)]
+    down = [(d, (d - 1) % ways) for d in range(ways)]
+    earlier, later = ([value], [value])
+    for _ in range(ways // 2):
+        earlier.append(lax.ppermute(earlier[-1], axis, up))
+    for _ in range((ways - 1) // 2):
+        later.append(lax.ppermute(later[-1], axis, down))
+    line = jnp.concatenate([*earlier[::-1], *later[1:]], axis=dim)
+    return jnp.roll(line, (lax.axis_index(axis) - ways // 2) * value.shape[dim], axis=dim)
 
 
 def on_device(
@@ -21,7 +34,7 @@
     row_blocks, per_tile = tile_columns.shape
     tile_rows = node_rows // row_blocks
     chosen = x_cached.reshape(row_blocks, tile_rows, width)[boundary_blocks[0]]
-    received = lax.all_gather(x_current, "grp", axis=0, tiled=True)
+    received = collect(x_current, "grp", 0)
     part_blocks = received.reshape(-1, tile_rows, width)
     partial_value = lax.all_gather(chosen[None, None], "grp", axis=1, tiled=True)
     halo_blocks = lax.all_gather(partial_value, "dom", axis=0, tiled=True)

time: 345 us -> 314 us (0.910); the launches traced: 343 us -> 308 us
  waiting for transfers between devices: 66.2 us -> 21.5 us
  local copies, waits for them, and re-layouts: 174 us -> 180 us
  starting transfers between devices: 0.04 us -> 3.75 us
    all_gather x1, waiting for transfers between devices: 49.4 us -> 0.01 us  [on_device(): halo_blocks = lax.all_gather(partial_value, 'dom', axis=0, tiled=True)]
    ppermute x0 -> x3, waiting for transfers between devices: none -> 21.5 us  [the longest x2 21.5 us: collect(): earlier.append(lax.ppermute(earlier[-1], axis, up))]
    all_gather x1 -> x0, waiting for transfers between devices: 16.1 us -> none  [on_device(): received = lax.all_gather(x_current, 'grp', axis=0, tiled=True)]
    ppermute x0 -> x3, starting transfers between devices: none -> 3.75 us  [the longest x1 2.67 us: collect(): later.append(lax.ppermute(later[-1], axis, down))]
    unnamed x17 -> x24, local copies, waits for them, and re-layouts: 20.7 us -> 24.3 us
  transfers between devices with their start and end apart: 2 -> 4, of which waited for: 2 -> 1; matrix products, arithmetic and copies ran while one was open for 7% -> 10% of each run, Pallas kernels for 0% -> 0%
where the time goes in v1:
time: 314 us; the launch traced here: 308 us
  local copies, waits for them, and re-layouts  180 us (57%)
  matrix products  61.1 us (19%)
  waiting for transfers between devices  21.5 us (7%)
  other arithmetic  15.6 us (5%)
  between operations  14.3 us (5%)
  blocking collectives  11.2 us (4%)
  starting transfers between devices  3.75 us (1%)
    gather x8, local copies, waits for them, and re-layouts, one_group(): gathered = block_table[columns]  89.3 us
    dot_general x8, matrix products, one_group(): jnp.einsum('stij,stjf->sif', adjacent, gathered, preferred_element_type=j...  50.1 us
    dynamic_slice x8, local copies, waits for them, and re-layouts, on_device(): lax.map(one_group, (tile_columns.reshape(turns, group_size, per_tile), ti...  35.8 us
    shift_right_arithmetic x24, local copies, waits for them, and re-layouts, one_group(): packed.reshape(group_size, per_tile, tile_rows, tile_rows // 8, 1) >> shifts  27.9 us
    unnamed x24, local copies, waits for them, and re-layouts  24.3 us
    ppermute x2, waiting for transfers between devices, collect(): earlier.append(lax.ppermute(earlier[-1], axis, up))  21.5 us
    all_gather x1, blocking collectives, on_device(): lax.all_gather(chosen[None, None], 'grp', axis=1, tiled=True)  11.2 us
    concatenate x1, other arithmetic, on_device(): jnp.concatenate([part_blocks, halo_blocks.reshape(-1, tile_rows, width)],...  7.4 us
  transfers between devices with their start and end apart: 4, of which 1 were waited for; matrix products, arithmetic and copies ran while one was open for 10% of the time, Pallas kernels for 0%

profile of v1, /device:TPU:1, one launch (start us, length us, event | category | flops | bytes accessed | tf_op | source)
XLA Modules:
  0.0 308.0 jit_solution(682831116496994700)
XLA Ops:
  7.8 11.2 %all-gather = bf16[4,128,128]{2,1,0:T(8,128)(2,1)} all-gather(bf16[1,128,128]{2,1,0:T(8,128)(2,1)S(1)} %constant_dynamic-slice_fusion.2), channel_id=2, replica_groups=mesh['dom'=32,'grp'=4] {'grp'}, dimensions={0}, use_global_device_ids=true | all-gather | bytes 163840 | tf_op jit(solution)/shard_map/all_gather | solution.py:39
  20.1 21.5 %collective-permute-done = bf16[4096,128]{1,0:T(8,128)(2,1)S(1)} collective-permute-done((bf16[4096,128]{1,0:T(8,128)(2,1)}, bf16[4096,128]{1,0:T(8,128)(2,1)S(1)}, u32[]{:S(2)}, u32[]{:S(2)}) %collective-permute-start) | collective-permute-done | bytes 1048608 | tf_op jit(solution)/shard_map/ppermute | solution.py:14
  44.3 20.5 %copy.16 = s32[32,40,2048]{1,2,0:T(8,128)} copy(s32[32,40,2048]{2,1,0:T(8,128)} %param.19) | data formatting | bytes 20971520 | tf_op args[7]
  75.0 7.4 %pad_maximum_fusion = bf16[256,128,128]{2,1,0:T(8,128)(2,1)} fusion(bf16[128,128,128]{2,1,0:T(8,128)(2,1)} %all-gather.4.cloned.1.call-done, bf16[128,128,128]{2,1,0:T(8,128)(2,1)} %bitcast.63), kind=kLoop, calls=%fused_computation.21 | loop fusion | flops 4194304 | bytes 16777216 | tf_op jit(solution)/shard_map/concatenate | solution.py:41
  82.4 210.1 %while.12 = (s32[]{:T(128)}, f32[8,4,128,128]{3,2,1,0:T(8,128)}, s32[8,4,40,2048]{2,3,1,0:T(8,128)}, s32[8,4]{1,0:T(8,128)S(1)}, s32[8,4,40]{2,1,0:T(4,128)}, /*index=5*/bf16[256,128,128]{2,1,0:T(8,128)(2,1)}, s32[]{:T(128)}) while((s32[]{:T(128)}, f32[8,4,128,128]{3,2,1,0:T(8,128)}, s32[8,4,40,2048]{2,3,1,0:T(8,128)}, ...), condition=%wide.region_1.2_spmd.clone, body=%wide.region_0.1_spmd.clone.sunk | while | flops 681576256 | bytes 22556296 | solution.py:61
  83.2 11.2 %gather_fusion = bf16[160,128,128]{2,1,0:T(8,128)(2,1)} fusion(bf16[256,128,128]{2,1,0:T(8,128)(2,1)} %get-tuple-element.136, s32[1024]{0:T(1024)S(1)} %pad_clamp_fusion.2), kind=kCustom, calls=%fused_computation.clone.clone.1 | custom fusion | bytes 10486400 | tf_op jit(solution)/shard_map/while/body/eval_jaxpr/gather | solution.py:58
  94.4 4.5 %constant_dynamic-slice_fusion.5 = s32[1,4,40,2048]{2,3,1,0:T(8,128)} fusion(s32[8,4,40,2048]{2,3,1,0:T(8,128)} %get-tuple-element.133, s32[]{:T(128)} %get-tuple-element.124), kind=kLoop, calls=%fused_computation.18.clone.1 | loop fusion | bytes 2621444 | tf_op jit(solution)/shard_map/while/body/jit(dynamic_index_in_dim)/dynamic_slice | solution.py:61
  102.4 6.3 %fusion.36 = f32[8,4,128,128]{3,2,1,0:T(8,128)} fusion(f32[8,4,128,128]{3,2,1,0:T(8,128)} %get-tuple-element.125, s32[]{:T(128)} %get-tuple-element.124, bf16[4,40,128,128]{3,2,1,0:T(8,128)(2,1)} %bitcast.61, s32[4,40]{1,0:T(4,128)S(1)} %fusion.35, s32[128]{0:T(128)S(1)} %shift_right_arithmetic.64, s32[4,40,128,16]{2,3,1,0:T(8,128)S(1)} %copy.20), kind=kOutput, calls=%fused_computation.12.clone.1 | convolution fusion | flops 681574400 | bytes 6817408 | tf_op jit(solution)/shard_map/while/body/eval_jaxpr/stij,stjf->sif/dot_general | solution.py:59
  109.5 11.2 %gather_fusion = bf16[160,128,128]{2,1,0:T(8,128)(2,1)} fusion(bf16[256,128,128]{2,1,0:T(8,128)(2,1)} %get-tuple-element.136, s32[1024]{0:T(1024)S(1)} %pad_clamp_fusion.2), kind=kCustom, calls=%fused_computation.clone.clone.1 | custom fusion | bytes 10486400 | tf_op jit(solution)/shard_map/while/body/eval_jaxpr/gather | solution.py:58
  120.6 4.5 %constant_dynamic-slice_fusion.5 = s32[1,4,40,2048]{2,3,1,0:T(8,128)} fusion(s32[8,4,40,2048]{2,3,1,0:T(8,128)} %get-tuple-element.133, s32[]{:T(128)} %get-tuple-element.124), kind=kLoop, calls=%fused_computation.18.clone.1 | loop fusion | bytes 2621444 | tf_op jit(solution)/shard_map/while/body/jit(dynamic_index_in_dim)/dynamic_slice | solution.py:61
  128.7 6.2 %fusion.36 = f32[8,4,128,128]{3,2,1,0:T(8,128)} fusion(f32[8,4,128,128]{3,2,1,0:T(8,128)} %get-tuple-element.125, s32[]{:T(128)} %get-tuple-element.124, bf16[4,40,128,128]{3,2,1,0:T(8,128)(2,1)} %bitcast.61, s32[4,40]{1,0:T(4,128)S(1)} %fusion.35, s32[128]{0:T(128)S(1)} %shift_right_arithmetic.64, s32[4,40,128,16]{2,3,1,0:T(8,128)S(1)} %copy.20), kind=kOutput, calls=%fused_computation.12.clone.1 | convolution fusion | flops 681574400 | bytes 6817408 | tf_op jit(solution)/shard_map/while/body/eval_jaxpr/stij,stjf->sif/dot_general | solution.py:59
  135.7 11.2 %gather_fusion = bf16[160,128,128]{2,1,0:T(8,128)(2,1)} fusion(bf16[256,128,128]{2,1,0:T(8,128)(2,1)} %get-tuple-element.136, s32[1024]{0:T(1024)S(1)} %pad_clamp_fusion.2), kind=kCustom, calls=%fused_computation.clone.clone.1 | custom fusion | bytes 10486400 | tf_op jit(solution)/shard_map/while/body/eval_jaxpr/gather | solution.py:58
  154.9 6.2 %fusion.36 = f32[8,4,128,128]{3,2,1,0:T(8,128)} fusion(f32[8,4,128,128]{3,2,1,0:T(8,128)} %get-tuple-element.125, s32[]{:T(128)} %get-tuple-element.124, bf16[4,40,128,128]{3,2,1,0:T(8,128)(2,1)} %bitcast.61, s32[4,40]{1,0:T(4,128)S(1)} %fusion.35, s32[128]{0:T(128)S(1)} %shift_right_arithmetic.64, s32[4,40,128,16]{2,3,1,0:T(8,128)S(1)} %copy.20), kind=kOutput, calls=%fused_computation.12.clone.1 | convolution fusion | flops 681574400 | bytes 6817408 | tf_op jit(solution)/shard_map/while/body/eval_jaxpr/stij,stjf->sif/dot_general | solution.py:59
  162.0 11.2 %gather_fusion = bf16[160,128,128]{2,1,0:T(8,128)(2,1)} fusion(bf16[256,128,128]{2,1,0:T(8,128)(2,1)} %get-tuple-element.136, s32[1024]{0:T(1024)S(1)} %pad_clamp_fusion.2), kind=kCustom, calls=%fused_computation.clone.clone.1 | custom fusion | bytes 10486400 | tf_op jit(solution)/shard_map/while/body/eval_jaxpr/gather | solution.py:58
  181.2 6.3 %fusion.36 = f32[8,4,128,128]{3,2,1,0:T(8,128)} fusion(f32[8,4,128,128]{3,2,1,0:T(8,128)} %get-tuple-element.125, s32[]{:T(128)} %get-tuple-element.124, bf16[4,40,128,128]{3,2,1,0:T(8,128)(2,1)} %bitcast.61, s32[4,40]{1,0:T(4,128)S(1)} %fusion.35, s32[128]{0:T(128)S(1)} %shift_right_arithmetic.64, s32[4,40,128,16]{2,3,1,0:T(8,128)S(1)} %copy.20), kind=kOutput, calls=%fused_computation.12.clone.1 | convolution fusion | flops 681574400 | bytes 6817408 | tf_op jit(solution)/shard_map/while/body/eval_jaxpr/stij,stjf->sif/dot_general | solution.py:59
  188.2 11.2 %gather_fusion = bf16[160,128,128]{2,1,0:T(8,128)(2,1)} fusion(bf16[256,128,128]{2,1,0:T(8,128)(2,1)} %get-tuple-element.136, s32[1024]{0:T(1024)S(1)} %pad_clamp_fusion.2), kind=kCustom, calls=%fused_computation.clone.clone.1 | custom fusion | bytes 10486400 | tf_op jit(solution)/shard_map/while/body/eval_jaxpr/gather | solution.py:58
  207.4 6.3 %fusion.36 = f32[8,4,128,128]{3,2,1,0:T(8,128)} fusion(f32[8,4,128,128]{3,2,1,0:T(8,128)} %get-tuple-element.125, s32[]{:T(128)} %get-tuple-element.124, bf16[4,40,128,128]{3,2,1,0:T(8,128)(2,1)} %bitcast.61, s32[4,40]{1,0:T(4,128)S(1)} %fusion.35, s32[128]{0:T(128)S(1)} %shift_right_arithmetic.64, s32[4,40,128,16]{2,3,1,0:T(8,128)S(1)} %copy.20), kind=kOutput, calls=%fused_computation.12.clone.1 | convolution fusion | flops 681574400 | bytes 6817408 | tf_op jit(solution)/shard_map/while/body/eval_jaxpr/stij,stjf->sif/dot_general | solution.py:59
  214.5 11.2 %gather_fusion = bf16[160,128,128]{2,1,0:T(8,128)(2,1)} fusion(bf16[256,128,128]{2,1,0:T(8,128)(2,1)} %get-tuple-element.136, s32[1024]{0:T(1024)S(1)} %pad_clamp_fusion.2), kind=kCustom, calls=%fused_computation.clone.clone.1 | custom fusion | bytes 10486400 | tf_op jit(solution)/shard_map/while/body/eval_jaxpr/gather | solution.py:58
  233.7 6.3 %fusion.36 = f32[8,4,128,128]{3,2,1,0:T(8,128)} fusion(f32[8,4,128,128]{3,2,1,0:T(8,128)} %get-tuple-element.125, s32[]{:T(128)} %get-tuple-element.124, bf16[4,40,128,128]{3,2,1,0:T(8,128)(2,1)} %bitcast.61, s32[4,40]{1,0:T(4,128)S(1)} %fusion.35, s32[128]{0:T(128)S(1)} %shift_right_arithmetic.64, s32[4,40,128,16]{2,3,1,0:T(8,128)S(1)} %copy.20), kind=kOutput, calls=%fused_computation.12.clone.1 | convolution fusion | flops 681574400 | bytes 6817408 | tf_op jit(solution)/shard_map/while/body/eval_jaxpr/stij,stjf->sif/dot_general | solution.py:59
  240.7 11.2 %gather_fusion = bf16[160,128,128]{2,1,0:T(8,128)(2,1)} fusion(bf16[256,128,128]{2,1,0:T(8,128)(2,1)} %get-tuple-element.136, s32[1024]{0:T(1024)S(1)} %pad_clamp_fusion.2), kind=kCustom, calls=%fused_computation.clone.clone.1 | custom fusion | bytes 10486400 | tf_op jit(solution)/shard_map/while/body/eval_jaxpr/gather | solution.py:58
  260.0 6.3 %fusion.36 = f32[8,4,128,128]{3,2,1,0:T(8,128)} fusion(f32[8,4,128,128]{3,2,1,0:T(8,128)} %get-tuple-element.125, s32[]{:T(128)} %get-tuple-element.124, bf16[4,40,128,128]{3,2,1,0:T(8,128)(2,1)} %bitcast.61, s32[4,40]{1,0:T(4,128)S(1)} %fusion.35, s32[128]{0:T(128)S(1)} %shift_right_arithmetic.64, s32[4,40,128,16]{2,3,1,0:T(8,128)S(1)} %copy.20), kind=kOutput, calls=%fused_computation.12.clone.1 | convolution fusion | flops 681574400 | bytes 6817408 | tf_op jit(solution)/shard_map/while/body/eval_jaxpr/stij,stjf->sif/dot_general | solution.py:59
  267.0 11.2 %gather_fusion = bf16[160,128,128]{2,1,0:T(8,128)(2,1)} fusion(bf16[256,128,128]{2,1,0:T(8,128)(2,1)} %get-tuple-element.136, s32[1024]{0:T(1024)S(1)} %pad_clamp_fusion.2), kind=kCustom, calls=%fused_computation.clone.clone.1 | custom fusion | bytes 10486400 | tf_op jit(solution)/shard_map/while/body/eval_jaxpr/gather | solution.py:58
  286.2 6.3 %fusion.36 = f32[8,4,128,128]{3,2,1,0:T(8,128)} fusion(f32[8,4,128,128]{3,2,1,0:T(8,128)} %get-tuple-element.125, s32[]{:T(128)} %get-tuple-element.124, bf16[4,40,128,128]{3,2,1,0:T(8,128)(2,1)} %bitcast.61, s32[4,40]{1,0:T(4,128)S(1)} %fusion.35, s32[128]{0:T(128)S(1)} %shift_right_arithmetic.64, s32[4,40,128,16]{2,3,1,0:T(8,128)S(1)} %copy.20), kind=kOutput, calls=%fused_computation.12.clone.1 | convolution fusion | flops 681574400 | bytes 6817408 | tf_op jit(solution)/shard_map/while/body/eval_jaxpr/stij,stjf->sif/dot_general | solution.py:59
  294.5 6.6 %maximum_convert_fusion = bf16[4096,512]{1,0:T(8,128)(2,1)} fusion(f32[4096,512]{1,0:T(8,128)} %fusion.21, bf16[4096,128]{1,0:T(8,128)(2,1)S(1)} %fusion.20, bf16[128,512]{1,0:T(8,128)(2,1)S(1)} %copy-done.4, f32[512]{0:T(512)S(1)} %copy-done.6), kind=kOutput, calls=%fused_computation.22 | convolution fusion | flops 545259520 | bytes 13764608 | tf_op jit(solution)/shard_map/dot_general | solution.py:73
  (109 shorter events, 78.1 us)
Async XLA Ops:
  6.5 1.2 copy-start
  6.5 68.5 %all-gather.4.cloned.1.call-start = ((), (), s32[]{:S(2)}) async-start(), calls=%async_computation | async-start | bytes 4325376 | tf_op jit(solution)/shard_map/all_gather | solution.py:40
  19.0 22.6 %collective-permute-start = (bf16[4096,128]{1,0:T(8,128)(2,1)}, bf16[4096,128]{1,0:T(8,128)(2,1)S(1)}, u32[]{:S(2)}, u32[]{:S(2)}) collective-permute-start(bf16[4096,128]{1,0:T(8,128)(2,1)} %param.12), channel_id=1, source_target_pairs={{0,1},{1,2},{2,3},{3,0},{4,5},{5,6},{6,7},{7,4},{8,9},{9,10},{10,1... | collective-permute-start | bytes 3145736 | tf_op jit(solution)/shard_map/ppermute | solution.py:14
  41.6 27.7 %collective-permute-start.1 = (bf16[4096,128]{1,0:T(8,128)(2,1)S(1)}, bf16[4096,128]{1,0:T(8,128)(2,1)}, u32[]{:S(2)}, u32[]{:S(2)}) collective-permute-start(bf16[4096,128]{1,0:T(8,128)(2,1)S(1)} %collective-permute-done), channel_id=1, source_target_pairs={{0,1},{1,2},{2,3},{3,0},{4,5},{5,6},{6,7},{7,4},{8,9},{9,10},{10,1... | collective-permute-start | bytes 3145736 | tf_op jit(solution)/shard_map/ppermute | solution.py:14
  41.6 29.3 %collective-permute-start.2 = (bf16[4096,128]{1,0:T(8,128)(2,1)}, bf16[4096,128]{1,0:T(8,128)(2,1)S(1)}, u32[]{:S(2)}, u32[]{:S(2)}) collective-permute-start(bf16[4096,128]{1,0:T(8,128)(2,1)} %param.12), channel_id=1, source_target_pairs={{0,3},{1,0},{2,1},{3,2},{4,7},{5,4},{6,5},{7,6},{8,11},{9,8},{10,9... | collective-permute-start | bytes 3145736 | tf_op jit(solution)/shard_map/ppermute | solution.py:16
  44.2 20.5 %copy-start.7 = (s32[32]{0:T(128)S(1)}, s32[32]{0:T(128)}, u32[]{:S(2)}) copy-start(s32[32]{0:T(128)} %param.18) | copy-start | bytes 388
  44.2 20.6 %copy-start.5 = (s32[4096]{0:T(1024)S(1)}, s32[4096]{0:T(1024)}, u32[]{:S(2)}) copy-start(s32[4096]{0:T(1024)} %param.20) | copy-start | bytes 49156
  44.2 20.6 %copy-start.2 = (bf16[4096,128]{1,0:T(8,128)(2,1)S(1)}, bf16[4096,128]{1,0:T(8,128)(2,1)}, u32[]{:S(2)}) copy-start(bf16[4096,128]{1,0:T(8,128)(2,1)} %param.12) | copy-start | bytes 3145732
  44.2 20.6 %copy-start.3 = (bf16[128,512]{1,0:T(8,128)(2,1)S(1)}, bf16[128,512]{1,0:T(8,128)(2,1)}, u32[]{:S(2)}) copy-start(bf16[128,512]{1,0:T(8,128)(2,1)} %param.14) | copy-start | bytes 393220
  82.4 212.1 %copy-start.4 = (bf16[128,512]{1,0:T(8,128)(2,1)S(1)}, bf16[128,512]{1,0:T(8,128)(2,1)}, u32[]{:S(2)}) copy-start(bf16[128,512]{1,0:T(8,128)(2,1)} %param.15) | copy-start | bytes 393220
  82.4 212.1 %copy-start.6 = (f32[512]{0:T(512)S(1)}, f32[512]{0:T(512)}, u32[]{:S(2)}) copy-start(f32[512]{0:T(512)} %param.16) | copy-start | bytes 6148
  292.5 8.7 %copy-start.1 = (bf16[4096,128]{1,0:T(8,128)(2,1)S(1)}, bf16[4096,128]{1,0:T(8,128)(2,1)}, u32[]{:S(2)}) copy-start(bf16[4096,128]{1,0:T(8,128)(2,1)} %param.13) | copy-start | bytes 3145732
Sparse Core Ops, SparseCore 0:
  19.1 51.3 all-gather.3
